TPU v7x, 32 devices: a whole 2x2x4 slice. The times are simulated.
32 devices in a mesh: groups: 2 (over y), gx: 16 (over z, x, core).
Axes of the slice: x: 2, y: 2, z: 4, core: 2. Of those that a mesh axis runs over, the one named last changes fastest.
Arguments:
- embeddings: bfloat16 [24576, 1024], P(('groups', 'gx')), parts along dimension 0, may hold values from -16 to 16
- membership: int32 [24576], P(('groups', 'gx')), parts along dimension 0, may hold values 0 or 1
Outputs:
- moved: bfloat16 [24576, 1024], P(('groups', 'gx')), parts along dimension 0
- relative: float32 [24576], P(('groups', 'gx')), parts along dimension 0
There are 2 independent parts, one for each index of `groups`. A program takes and returns all parts, laid end to end along the dimension named above; each array names one. Nothing has to cross between parts.
All inputs are finite; a program needn't handle non-finite values. No bound on the sum of `membership` on one device may be relied on, other than what follows from the above.
Results may differ from a plain program's by a relative error of at most 0.001.
Values may be sent and summed in bfloat16 or wider, within the bound.
A program may use at most 64 MiB of HBM per device.

v0:
```python
import jax
import jax.numpy as jnp
from jax import lax
from jax.sharding import PartitionSpec as P


def shifted(shard, axis, by):
    devices = lax.axis_size(axis)
    return lax.ppermute(shard, axis, [(i, (i + by) % devices) for i in range(devices)])


def kernel_block(rows, row_norms, keys, key_norms):
    width = rows.shape[1]
    dots = lax.dot_general(rows, keys, (((1,), (1,)), ((), ())), preferred_element_type=jnp.float32)
    dist = row_norms[:, None] + key_norms[None, :] - 2.0 * dots
    return jnp.exp(-(4.0 / width) * dist)


def row_terms(raw, keys, key_member):
    weight = raw * key_member[None, :]
    sums = jnp.dot(weight.astype(jnp.bfloat16), keys, preferred_element_type=jnp.float32)
    return (jnp.sum(weight, axis=1), sums)


def square_norms(rows):
    return jnp.sum(jnp.square(rows.astype(jnp.float32)), axis=1)


def shards(embeddings, membership):
    count = lax.axis_size("gx")
    first = count // 4
    second = 3 * count // 8
    member = membership.astype(jnp.float32)
    member_low = member.astype(jnp.bfloat16)
    norms = square_norms(embeddings)
    raw = kernel_block(embeddings, norms, embeddings, norms)
    density, sums = row_terms(raw, embeddings, member)
    for distance in (first, second):
        keys, key_flags = shifted((embeddings, member_low), "gx", -distance)
        key_member = key_flags.astype(jnp.float32)
        key_norms = square_norms(keys)
        raw = kernel_block(embeddings, norms, keys, key_norms)
        part_density, part_sums = row_terms(raw, keys, key_member)
        density = density + part_density
        sums = sums + part_sums
        back_keys, back_flags = shifted((embeddings, member_low), "gx", distance)
        back_norms = square_norms(back_keys)
        back_raw = kernel_block(embeddings, norms, back_keys, back_norms)
        back_density, back_sums = row_terms(back_raw, back_keys, back_flags.astype(jnp.float32))
        density = density + back_density
        sums = sums + back_sums
    moved = (sums / jnp.maximum(density, 1.0)[:, None]).astype(jnp.bfloat16)
    member_density, member_count = lax.psum((jnp.sum(density * member), jnp.sum(member)), "gx")
    relative = density / (1.0 + member_density / jnp.maximum(member_count, 1.0))
    return (moved, relative)


def solution(mesh):
    in_specs = (P(("groups", "gx"), None), P(("groups", "gx")))
    out_specs = (P(("groups", "gx"), None), P(("groups", "gx")))
    return jax.shard_map(shards, mesh=mesh, in_specs=in_specs, out_specs=out_specs, check_vma=False)
```

profile of v0, /device:TPU:0, one launch (start us, length us, event | category | flops | bytes accessed | tf_op | source)
XLA Modules:
  0.0 236.1 jit_solution(12581899860029859425)
XLA Ops:
  0.6 4.0 %collective-permute-start.6 = (bf16[768,1024]{1,0:T(8,128)(2,1)}, bf16[768,1024]{1,0:T(8,128)(2,1)S(1)}, u32[]{:S(2)}, u32[]{:S(2)}) collective-permute-start(bf16[768,1024]{1,0:T(8,128)(2,1)} %param.2), channel_id=1, source_target_pairs={{0,6},{1,7},{2,8},{3,9},{4,10},{5,11},{6,12},{7,13},{8,14},{9,15},... | collective-permute-start | bytes 4718600 | tf_op jit(solution)/shard_map/ppermute | solution.py:9
  4.6 1.1 collective-permute-start.4
  5.7 1.8 collective-permute-start.2
  7.5 0.7 fusion.48
  8.2 2.0 collective-permute-start.1
  10.3 1.8 multiply_reduce_fusion.4
  12.0 0.0 copy-start
  12.0 3.7 %fusion.49 = (f32[768]{0:T(1024)S(1)}, bf16[768,768]{0,1:T(8,128)(2,1)S(1)}) fusion(f32[768]{0:T(1024)S(1)} %get-tuple-element.13, bf16[768,1024]{1,0:T(8,128)(2,1)} %param.2, f32[768]{0:T(1024)S(1)} %multiply_reduce_fusion.4), kind=kOutput, calls=%fused_computation.60 | convolution fusion | flops 1212087552 | bytes 2761728 | tf_op jit(solution)/shard_map/dot_general | solution.py:14
  15.8 90.3 %collective-permute-done.1 = bf16[768]{0:T(1024)(128)(2,1)S(1)} collective-permute-done((bf16[768]{0:T(1024)(128)(2,1)S(1)}, bf16[768]{0:T(1024)(128)(2,1)S(1)}, u32[]{:S(2)}, u32[]{:S(2)}) %collective-permute-start.1) | collective-permute-done | bytes 1568 | tf_op jit(solution)/shard_map/ppermute | solution.py:9
  106.1 35.0 %collective-permute-start.5 = (bf16[768]{0:T(1024)(128)(2,1)S(1)}, bf16[768]{0:T(1024)(128)(2,1)S(1)}, u32[]{:S(2)}, u32[]{:S(2)}) collective-permute-start(bf16[768]{0:T(1024)(128)(2,1)S(1)} %get-tuple-element.14), channel_id=1, source_target_pairs={{0,10},{1,11},{2,12},{3,13},{4,14},{5,15},{6,0},{7,1},{8,2},{9,3},... | collective-permute-start | bytes 4616 | tf_op jit(solution)/shard_map/ppermute | solution.py:9
  141.1 1.2 collective-permute-start.7
  142.3 3.1 %fusion.26 = f32[768,1024]{1,0:T(8,128)} fusion(bf16[768,1024]{1,0:T(8,128)(2,1)S(1)} %copy-done, bf16[768,768]{0,1:T(8,128)(2,1)S(1)} %get-tuple-element.17), kind=kOutput, calls=%fused_computation.31 | convolution fusion | flops 1207959552 | bytes 5898240 | tf_op jit(solution)/shard_map/dot_general | solution.py:21
  145.5 2.2 collective-permute-start
  147.6 0.4 multiply_reduce_fusion
  148.0 0.4 multiply_reduce_fusion.1
  148.4 0.4 multiply_reduce_fusion.2
  148.8 1.4 fusion.50
  150.3 1.4 fusion.51
  151.7 1.4 fusion.52
  153.1 29.7 %collective-permute-done = bf16[768,1024]{1,0:T(8,128)(2,1)S(1)} collective-permute-done((bf16[768,1024]{1,0:T(8,128)(2,1)S(1)}, bf16[768,1024]{1,0:T(8,128)(2,1)S(1)}, u32[]{:S(2)}, u32[]{:S(2)}) %collective-permute-start) | collective-permute-done | bytes 1572896 | tf_op jit(solution)/shard_map/ppermute | solution.py:9
  182.8 0.4 multiply_reduce_fusion.3
  183.2 5.5 %fusion = (f32[768]{0:T(1024)S(1)}, f32[768]{0:T(1024)S(1)}, f32[768]{0:T(1024)S(1)}, f32[768]{0:T(1024)S(1)}, f32[768,768]{0,1:T(8,128)}) fusion(f32[768]{0:T(1024)S(1)} %convert_element_type.56, f32[768]{0:T(1024)S(1)} %multiply_reduce_fusion.3, f32[768]{0:T(1024)S(1)} %multiply_reduce_fusion.4, f32[768]{0:T(1024)S(1)} %convert_element_type.59, ...), kind=kOutput, calls=%fused_computation.11 | convolution fusion | flops 1222112256 | bytes 12622848 | tf_op jit(solution)/shard_map/dot_general | solution.py:14
  188.7 0.6 convert_reduce_fusion
  189.3 32.6 %all-reduce = (f32[]{:T(128)}, f32[]{:T(128)}) all-reduce(f32[]{:T(128)} %get-tuple-element.3, f32[]{:T(128)} %get-tuple-element.2), channel_id=1, replica_groups=mesh['groups'=2,'gx'=16] {'gx'}, use_global_device_ids=true, to_apply=%region_11.0 | all-reduce | flops 2 | bytes 16 | tf_op jit(solution)/shard_map/psum | solution.py:53
  223.2 0.6 broadcast_divide_fusion
  223.8 4.0 %fusion.14 = f32[768,1024]{1,0:T(8,128)S(1)} fusion(bf16[768,1024]{1,0:T(8,128)(2,1)} %copy-done.1, f32[768,768]{0,1:T(8,128)} %copy-done.10, f32[768]{0:T(1024)S(1)} %convert_element_type.59, f32[768]{0:T(1024)S(1)} %multiply_reduce_fusion.2, f32[768]{0:T(1024)S(1)} %multiply_reduce_fusion.4), kind=kOutput, calls=%fused_computation.21 | convolution fusion | flops 1211498496 | bytes 7087104 | tf_op jit(solution)/shard_map/dot_general | solution.py:21
  227.8 1.7 fusion.12
  229.5 0.4 copy-done.11
  229.9 1.8 fusion.16
  231.7 0.1 copy-done.5
  231.8 0.7 copy-done.7
  232.6 3.5 %divide_convert_fusion = bf16[768,1024]{1,0:T(8,128)(2,1)} fusion(f32[768,1024]{1,0:T(8,128)S(1)} %fusion.12, f32[768,1024]{1,0:T(8,128)S(1)} %fusion.14, f32[768,1024]{1,0:T(8,128)S(1)} %copy-done.5, f32[768,1024]{1,0:T(8,128)S(1)} %fusion.16, f32[768]{0:T(1024)S(1)} %get-tuple-element.12, bf16[768,1024]{1,0:T(8,128)(2,1)S(1)} %collective-permute-done.6, ...), kind=kOutput, calls=%fused_computation | convolution fusion | flops 1216217088 | bytes 18100224 | tf_op jit(solution)/shard_map/dot_general | solution.py:21
  (31 shorter events, 0.1 us)
Async XLA Ops:
  0.6 147.0 %collective-permute-start.6 = (bf16[768,1024]{1,0:T(8,128)(2,1)}, bf16[768,1024]{1,0:T(8,128)(2,1)S(1)}, u32[]{:S(2)}, u32[]{:S(2)}) collective-permute-start(bf16[768,1024]{1,0:T(8,128)(2,1)} %param.2), channel_id=1, source_target_pairs={{0,6},{1,7},{2,8},{3,9},{4,10},{5,11},{6,12},{7,13},{8,14},{9,15},... | collective-permute-start | bytes 4718600 | tf_op jit(solution)/shard_map/ppermute | solution.py:9
  4.6 143.4 %collective-permute-start.4 = (bf16[768,1024]{1,0:T(8,128)(2,1)}, bf16[768,1024]{1,0:T(8,128)(2,1)S(1)}, u32[]{:S(2)}, u32[]{:S(2)}) collective-permute-start(bf16[768,1024]{1,0:T(8,128)(2,1)} %param.2), channel_id=1, source_target_pairs={{0,10},{1,11},{2,12},{3,13},{4,14},{5,15},{6,0},{7,1},{8,2},{9,3},... | collective-permute-start | bytes 4718600 | tf_op jit(solution)/shard_map/ppermute | solution.py:9
  5.7 142.7 %collective-permute-start.2 = (bf16[768,1024]{1,0:T(8,128)(2,1)}, bf16[768,1024]{1,0:T(8,128)(2,1)S(1)}, u32[]{:S(2)}, u32[]{:S(2)}) collective-permute-start(bf16[768,1024]{1,0:T(8,128)(2,1)} %param.2), channel_id=1, source_target_pairs={{0,4},{1,5},{2,6},{3,7},{4,8},{5,9},{6,10},{7,11},{8,12},{9,13},{1... | collective-permute-start | bytes 4718600 | tf_op jit(solution)/shard_map/ppermute | solution.py:9
  8.2 97.9 %collective-permute-start.1 = (bf16[768]{0:T(1024)(128)(2,1)S(1)}, bf16[768]{0:T(1024)(128)(2,1)S(1)}, u32[]{:S(2)}, u32[]{:S(2)}) collective-permute-start(bf16[768]{0:T(1024)(128)(2,1)S(1)} %get-tuple-element.14), channel_id=1, source_target_pairs={{0,12},{1,13},{2,14},{3,15},{4,0},{5,1},{6,2},{7,3},{8,4},{9,5},{1... | collective-permute-start | bytes 4616 | tf_op jit(solution)/shard_map/ppermute | solution.py:9
  10.2 130.9 %collective-permute-start.3 = (bf16[768]{0:T(1024)(128)(2,1)S(1)}, bf16[768]{0:T(1024)(128)(2,1)S(1)}, u32[]{:S(2)}, u32[]{:S(2)}) collective-permute-start(bf16[768]{0:T(1024)(128)(2,1)S(1)} %get-tuple-element.14), channel_id=1, source_target_pairs={{0,4},{1,5},{2,6},{3,7},{4,8},{5,9},{6,10},{7,11},{8,12},{9,13},{1... | collective-permute-start | bytes 4616 | tf_op jit(solution)/shard_map/ppermute | solution.py:9
  12.0 130.3 %copy-start = (bf16[768,1024]{1,0:T(8,128)(2,1)S(1)}, bf16[768,1024]{1,0:T(8,128)(2,1)}, u32[]{:S(2)}) copy-start(bf16[768,1024]{1,0:T(8,128)(2,1)} %param.2) | copy-start | bytes 4718596
  106.1 39.3 %collective-permute-start.5 = (bf16[768]{0:T(1024)(128)(2,1)S(1)}, bf16[768]{0:T(1024)(128)(2,1)S(1)}, u32[]{:S(2)}, u32[]{:S(2)}) collective-permute-start(bf16[768]{0:T(1024)(128)(2,1)S(1)} %get-tuple-element.14), channel_id=1, source_target_pairs={{0,10},{1,11},{2,12},{3,13},{4,14},{5,15},{6,0},{7,1},{8,2},{9,3},... | collective-permute-start | bytes 4616 | tf_op jit(solution)/shard_map/ppermute | solution.py:9
  141.1 6.5 %collective-permute-start.7 = (bf16[768]{0:T(1024)(128)(2,1)S(1)}, bf16[768]{0:T(1024)(128)(2,1)S(1)}, u32[]{:S(2)}, u32[]{:S(2)}) collective-permute-start(bf16[768]{0:T(1024)(128)(2,1)S(1)} %get-tuple-element.14), channel_id=1, source_target_pairs={{0,6},{1,7},{2,8},{3,9},{4,10},{5,11},{6,12},{7,13},{8,14},{9,15},... | collective-permute-start | bytes 4616 | tf_op jit(solution)/shard_map/ppermute | solution.py:9
  145.5 37.3 %collective-permute-start = (bf16[768,1024]{1,0:T(8,128)(2,1)S(1)}, bf16[768,1024]{1,0:T(8,128)(2,1)S(1)}, u32[]{:S(2)}, u32[]{:S(2)}) collective-permute-start(bf16[768,1024]{1,0:T(8,128)(2,1)S(1)} %copy-done), channel_id=1, source_target_pairs={{0,12},{1,13},{2,14},{3,15},{4,0},{5,1},{6,2},{7,3},{8,4},{9,5},{1... | collective-permute-start | bytes 4718600 | tf_op jit(solution)/shard_map/ppermute | solution.py:9
  148.4 1.8 copy-start.1
  150.2 32.9 %copy-start.10 = (f32[768,768]{0,1:T(8,128)}, f32[768,768]{0,1:T(8,128)S(1)}, u32[]{:S(2)}) copy-start(f32[768,768]{0,1:T(8,128)S(1)} %fusion.50) | copy-start | bytes 7077892
  151.7 31.5 %copy-start.8 = (f32[768,768]{0,1:T(8,128)}, f32[768,768]{0,1:T(8,128)S(1)}, u32[]{:S(2)}) copy-start(f32[768,768]{0,1:T(8,128)S(1)} %fusion.51) | copy-start | bytes 7077892
  153.1 35.6 %copy-start.6 = (f32[768,768]{0,1:T(8,128)}, f32[768,768]{0,1:T(8,128)S(1)}, u32[]{:S(2)}) copy-start(f32[768,768]{0,1:T(8,128)S(1)} %fusion.52) | copy-start | bytes 7077892
  182.8 5.9 %copy-start.2 = (bf16[768,1024]{1,0:T(8,128)(2,1)}, bf16[768,1024]{1,0:T(8,128)(2,1)S(1)}, u32[]{:S(2)}) copy-start(bf16[768,1024]{1,0:T(8,128)(2,1)S(1)} %collective-permute-done) | copy-start | bytes 4718596
  183.2 5.5 %copy-start.4 = (s32[768]{0:T(1024)S(1)}, s32[768]{0:T(1024)}, u32[]{:S(2)}) copy-start(s32[768]{0:T(1024)} %param.3) | copy-start | bytes 9220
  223.8 4.0 %copy-start.9 = (f32[768,768]{0,1:T(8,128)S(1)}, f32[768,768]{0,1:T(8,128)}, u32[]{:S(2)}) copy-start(f32[768,768]{0,1:T(8,128)} %copy-done.8) | copy-start | bytes 7077892
  227.8 1.8 copy-start.3
  227.8 2.1 copy-start.11
  229.9 1.9 copy-start.5
  229.9 2.6 %copy-start.7 = (f32[768,768]{0,1:T(8,128)S(1)}, f32[768,768]{0,1:T(8,128)}, u32[]{:S(2)}) copy-start(f32[768,768]{0,1:T(8,128)} %copy-done.6) | copy-start | bytes 7077892
where the time goes:
time: 236 us
  waiting for transfers between devices  120 us (51%)
  starting transfers between devices  47.3 us (20%)
  blocking collectives  32.6 us (14%)
  matrix products  27.5 us (12%)
  other arithmetic  5.21 us (2%)
    ppermute x8, waiting for transfers between devices, shifted(): lax.ppermute(shard, axis, [(i, (i + by) % devices) for i in range(devices)])  120 us
    ppermute x8, starting transfers between devices, shifted(): lax.ppermute(shard, axis, [(i, (i + by) % devices) for i in range(devices)])  47.3 us
    psum x1, blocking collectives, shards(): lax.psum((jnp.sum(density * member), jnp.sum(member)), 'gx')  32.6 us
    dot_general x5, matrix products, row_terms(): jnp.dot(weight.astype(jnp.bfloat16), keys, preferred_element_type=jnp.flo...  14.1 us
    dot_general x5, matrix products, kernel_block(): lax.dot_general(rows, keys, (((1,), (1,)), ((), ())), preferred_element_t...  13.5 us
  transfers between devices with their start and end apart: 8, of which 2 were waited for; matrix products, arithmetic and copies ran while one was open for 6% of the time, Pallas kernels for 0%

commit v1 on v0

v1 whole, which is shorter than its diff:
```python
import functools

import jax
import jax.numpy as jnp
from jax import lax
from jax.experimental import pallas as pl
from jax.experimental.pallas import tpu as pltpu
from jax.sharding import PartitionSpec as P

MESH = pl.DeviceIdType.MESH
CHUNK = 64
LAG = 2
TILE = 384
LANES = 128


def plan(chunks, lag):
    half = chunks // 2
    low, high = list(range(half)), list(range(half, chunks))
    ahead, behind = low + high, high + low
    ready = {}
    done_x, done_pass_a, done_pass_b = set(), set(), set()
    slots = []
    t = 0
    while ahead or behind or len(done_x) < chunks + half or len(done_pass_a) < half or len(done_pass_b) < half:
        now = {key for key, when in ready.items() if when <= t}
        sends = {}
        passed = [k for k in high if (5, k) in now and k not in done_pass_b]
        if passed:
            done_pass_b.add(passed[0])
            sends["ahead"] = ("pass", passed[0])
        elif ahead:
            sends["ahead"] = ("own", ahead.pop(0))
        passed = [k for k in low if (3, k) in now and k not in done_pass_a]
        if passed:
            done_pass_a.add(passed[0])
            sends["behind"] = ("pass", passed[0])
        elif behind:
            sends["behind"] = ("own", behind.pop(0))
        order = [role_chunk for pair in zip([(1, k) for k in low], [(2, k) for k in high]) for role_chunk in pair]
        order += [(1, k) for k in high]
        across = [rc for rc in order if rc in now and rc not in done_x]
        if across:
            done_x.add(across[0])
            sends["across"] = across[0]
        for link, what in sends.items():
            if link == "across":
                key = (3, what[1]) if what[0] == 1 else (5, what[1])
            elif what[0] == "own":
                key = (1, what[1]) if link == "ahead" else (2, what[1])
            else:
                key = (4, what[1])
            ready[key] = t + lag
        slots.append(sends)
        t += 1
    return slots, ready


def kernel(count, e_ref, member_ref, moved_ref, density_ref, held, passing, bias, bias_col, sums, dens,
           recv, send_own, send_x, send_pass, bias_send, bias_recv):
    rows, width = e_ref.shape
    chunks = rows // CHUNK
    half = chunks // 2
    tile = TILE if rows % TILE == 0 else rows
    scale = 4.0 / width
    unit = count // 8
    me = lax.axis_index("gx")
    z = lax.div(me, 2 * unit)
    x = lax.rem(lax.div(me, unit), 2)
    rest = lax.rem(me, unit)
    step = 1 - 2 * x

    def device(up, side):
        return (lax.rem(z + up + 4, 4) * 2 + side) * unit + rest

    ahead = device(step, x)
    behind = device(-step, x)
    across = device(0, 1 - x)
    diagonal = device(step, 1 - x)
    opposite = device(2, 1 - x)

    barrier = pltpu.get_barrier_semaphore()
    for other in (ahead, behind, across, diagonal, opposite):
        pl.semaphore_signal(barrier, inc=1, device_id={"gx": other}, device_id_type=MESH)
    pl.semaphore_wait(barrier, 5)

    def piece(role, k):
        if role == 0:
            return e_ref.at[pl.ds(k * CHUNK, CHUNK)]
        if role == 5:
            return passing.at[pl.ds((k - half) * CHUNK, CHUNK)]
        return held.at[role - 1, pl.ds(k * CHUNK, CHUNK)]

    def copy(source, target, k, sem, other):
        return pltpu.make_async_remote_copy(
            src_ref=piece(source, k), dst_ref=piece(target, k), send_sem=sem, recv_sem=recv.at[target - 1, k],
            device_id={"gx": other}, device_id_type=MESH)

    slots, ready = plan(chunks, LAG)
    copies = []
    arrived = {}

    def wait_for(role, k):
        if (role, k) not in arrived:
            arrived[(role, k)] = True
            copy(role, role, k, send_own.at[0, 0], across).wait_recv()

    def issue(sends):
        for link in ("across", "ahead", "behind"):
            if link not in sends:
                continue
            kind, k = sends[link]
            if link == "across":
                wait_for(kind, k)
                made = copy(kind, 3 if kind == 1 else 5, k, send_x.at[kind - 1, k], across)
            elif kind == "own":
                lane = 0 if link == "ahead" else 1
                made = copy(0, 1 + lane, k, send_own.at[lane, k], ahead if lane == 0 else behind)
            else:
                source = 5 if link == "ahead" else 3
                wait_for(source, k)
                made = copy(source, 4, k, send_pass.at[k], ahead if link == "ahead" else behind)
            made.start()
            copies.append(made)

    def prepare():
        @pl.loop(0, rows // LANES)
        def _(i):
            at = pl.ds(pl.multiple_of(i * LANES, LANES), LANES)
            values = e_ref[at, :].astype(jnp.float32)
            norms = jnp.sum(values * values, axis=1, keepdims=True) * scale
            wide = jnp.broadcast_to(norms, (LANES, LANES))
            bias_col[at, :] = wide
            line = jnp.transpose(wide)[0:1, :]
            bias[0, :, at] = jnp.where(member_ref[:, at] > 0, line, 1e30)
            dens[at, :] = jnp.zeros((LANES, LANES), jnp.float32)

    def compute(role, start, size, first=False):
        @pl.loop(0, rows // 256)
        def _(i):
            at = pl.ds(pl.multiple_of(i * 256, 256), 256)
            keys = e_ref[start:start + size, :] if role == 0 else held[role - 1, start:start + size, :]
            dots = lax.dot_general(e_ref[at, :], keys, (((1,), (1,)), ((), ())), preferred_element_type=jnp.float32)
            own = bias_col[at, :]
            total = dens[at, :]
            parts = []
            for j in range(0, size, LANES):
                dist = own + bias[role, :, start + j:start + j + LANES]
                weight = jnp.exp(2.0 * scale * dots[:, j:j + LANES] - dist)
                total = total + weight
                parts.append(weight.astype(jnp.bfloat16))
            dens[at, :] = total
            low = jnp.concatenate(parts, axis=1) if len(parts) > 1 else parts[0]
            term = jnp.dot(low, keys, preferred_element_type=jnp.float32)
            if first:
                sums[at, :] = term
            else:
                sums[at, :] += term

    def bias_copy(role, other):
        return pltpu.make_async_remote_copy(
            src_ref=bias.at[0], dst_ref=bias.at[role], send_sem=bias_send.at[role - 1], recv_sem=bias_recv.at[role - 1],
            device_id={"gx": other}, device_id_type=MESH)

    bias_ready = set()

    def need_bias(role):
        if role > 0 and role not in bias_ready:
            bias_ready.add(role)
            bias_copy(role, across).wait_recv()

    tiles = []
    for role in range(1, 5):
        for start in range(0, rows, tile):
            ks = range(start // CHUNK, (start + tile) // CHUNK)
            tiles.append((max(ready[(role, k)] for k in ks), role, start))
    tiles.sort()
    own_tiles = list(range(0, rows, tile))

    for t in range(LAG):
        issue(slots[t])
    prepare()
    for role, other in ((1, ahead), (2, behind), (3, diagonal), (4, opposite)):
        made = bias_copy(role, other)
        made.start()
        copies.append(made)

    last = max(ready.values())
    for t in range(LAG, last + 1):
        for key, when in ready.items():
            if when == t:
                wait_for(*key)
        if t < len(slots):
            issue(slots[t])
        if own_tiles:
            start = own_tiles.pop(0)
            compute(0, start, tile, first=start == 0)
        elif tiles and tiles[0][0] <= t:
            _, role, start = tiles.pop(0)
            need_bias(role)
            compute(role, start, tile)
    for _, role, start in tiles:
        need_bias(role)
        compute(role, start, tile)

    @pl.loop(0, rows // LANES)
    def _(i):
        at = pl.ds(pl.multiple_of(i * LANES, LANES), LANES)
        density = jnp.sum(dens[at, :], axis=1, keepdims=True)
        wide = jnp.broadcast_to(density, (LANES, LANES))
        density_ref[:, at] = jnp.transpose(wide)[0:1, :]
        moved_ref[at, :] = (sums[at, :] / jnp.maximum(density, 1.0)).astype(moved_ref.dtype)

    for made in copies:
        made.wait_send()


def shards(count, embeddings, membership):
    rows, width = embeddings.shape
    chunks = rows // CHUNK
    vmem = pl.BlockSpec(memory_space=pltpu.VMEM)
    moved, density = pl.pallas_call(
        functools.partial(kernel, count),
        out_shape=(jax.ShapeDtypeStruct((rows, width), jnp.bfloat16), jax.ShapeDtypeStruct((1, rows), jnp.float32)),
        in_specs=[vmem, vmem],
        out_specs=(vmem, vmem),
        scratch_shapes=[
            pltpu.VMEM((4, rows, width), jnp.bfloat16),
            pltpu.VMEM((rows // 2, width), jnp.bfloat16),
            pltpu.VMEM((5, 1, rows), jnp.float32),
            pltpu.VMEM((rows, LANES), jnp.float32),
            pltpu.VMEM((rows, width), jnp.float32),
            pltpu.VMEM((rows, LANES), jnp.float32),
            pltpu.SemaphoreType.DMA((5, chunks)),
            pltpu.SemaphoreType.DMA((2, chunks)),
            pltpu.SemaphoreType.DMA((2, chunks)),
            pltpu.SemaphoreType.DMA((chunks,)),
            pltpu.SemaphoreType.DMA((4,)),
            pltpu.SemaphoreType.DMA((4,)),
        ],
        compiler_params=pltpu.CompilerParams(collective_id=0, has_side_effects=True, vmem_limit_bytes=48 * 1024 * 1024),
    )(embeddings, membership[None, :])
    density = density[0]
    member = membership.astype(jnp.float32)
    member_density, member_count = lax.psum((jnp.sum(density * member), jnp.sum(member)), "gx")
    relative = density / (1.0 + member_density / jnp.maximum(member_count, 1.0))
    return (moved, relative)


def solution(mesh):
    in_specs = (P(("groups", "gx"), None), P(("groups", "gx")))
    out_specs = (P(("groups", "gx"), None), P(("groups", "gx")))
    step = functools.partial(shards, mesh.shape["gx"])
    return jax.shard_map(step, mesh=mesh, in_specs=in_specs, out_specs=out_specs, check_vma=False)
```

time: 236 us -> 155 us (0.66)
  waiting for transfers between devices: 120 us -> 0 us
  Pallas kernels: 0 us -> 118 us
  starting transfers between devices: 47.3 us -> 0 us
  matrix products: 27.5 us -> 0 us
  other arithmetic: 5.21 us -> 1.22 us
  blocking collectives: 32.6 us -> 30.1 us
    ppermute x8 -> x0, waiting for transfers between devices: 120 us -> none  [shifted(): lax.ppermute(shard, axis, [(i, (i + by) % devices) for i in range(devices)])]
    pallas_call x0 -> x1, Pallas kernels: none -> 118 us  [shards(): pl.pallas_call(functools.partial(kernel, count), out_shape=(jax.ShapeDtyp...]
    ppermute x8 -> x0, starting transfers between devices: 47.3 us -> none  [shifted(): lax.ppermute(shard, axis, [(i, (i + by) % devices) for i in range(devices)])]
    dot_general x10 -> x0, matrix products: 27.5 us -> none  [the longest x5 14.1 us: row_terms(): jnp.dot(weight.astype(jnp.bfloat16), keys, preferred_element_type=jnp.flo...]
    reduce_sum x5 -> x0, other arithmetic: 3.28 us -> none  [square_norms(): return jnp.sum(jnp.square(rows.astype(jnp.float32)), axis=1)]
    psum x1, blocking collectives: 32.6 us -> 30.1 us  [shards(): lax.psum((jnp.sum(density * member), jnp.sum(member)), 'gx')]
  transfers between devices with their start and end apart: 8 -> 0, of which waited for: 2 -> 0; matrix products, arithmetic and copies ran while one was open for 6% -> 0% of each run, Pallas kernels for 0% -> 0%
where the time goes in v1:
time: 155 us
  Pallas kernels  118 us (76%)
  blocking collectives  30.1 us (19%)
  local copies, waits for them, and re-layouts  3.31 us (2%)
  between operations  1.97 us (1%)
    pallas_call x1, Pallas kernels, shards(): pl.pallas_call(functools.partial(kernel, count), out_shape=(jax.ShapeDtyp...  118 us
    psum x1, blocking collectives, shards(): lax.psum((jnp.sum(density * member), jnp.sum(member)), 'gx')  30.1 us

profile of v1, /device:TPU:0, one launch (start us, length us, event | category | flops | bytes accessed | tf_op | source)
XLA Modules:
  0.0 154.7 jit_solution(13030828207873203784)
XLA Ops:
  0.6 0.0 copy-start.1
  0.6 0.8 broadcast_in_dim.3.member_ref
  1.4 0.0 copy-start
  1.4 1.4 copy-done
  2.8 118.1 %shard_map.41 = (bf16[768,1024]{1,0:T(8,128)(2,1)S(1)}, f32[1,768]{1,0:T(1,128)S(1)}) custom-call(bf16[768,1024]{1,0:T(8,128)(2,1)S(1)} %copy-done, s32[1,768]{1,0:T(1,128)S(1)} %broadcast_in_dim.3.member_ref), custom_call_target="tpu_custom_call" | custom-call | tf_op jit(solution)/shard_map/pallas_call | solution.py:222
  120.9 0.0 copy-done.1
  120.9 0.6 convert_reduce_fusion
  121.5 30.1 %all-reduce = (f32[]{:T(128)}, f32[]{:T(128)}) all-reduce(f32[]{:T(128)} %get-tuple-element.7, f32[]{:T(128)} %get-tuple-element.6), channel_id=1, replica_groups=mesh['groups'=2,'gx'=16] {'gx'}, use_global_device_ids=true, to_apply=%region_1.0 | all-reduce | flops 2 | bytes 16 | tf_op jit(solution)/shard_map/psum | solution.py:245
  152.9 0.6 broadcast_divide_fusion
  153.5 1.1 copy.5
  (1 shorter events, 0.0 us)
Async XLA Ops:
  0.6 120.3 %copy-start.1 = (s32[768]{0:T(1024)S(1)}, s32[768]{0:T(1024)}, u32[]{:S(2)}) copy-start(s32[768]{0:T(1024)} %param.3) | copy-start | bytes 9220
  1.4 1.4 copy-start

commit v2 on v1

--- a/solution.py
+++ b/solution.py
@@ -56,8 +56,17 @@
     return slots, ready
 
 
-def kernel(count, e_ref, member_ref, moved_ref, density_ref, held, passing, bias, bias_col, sums, dens,
-           recv, send_own, send_x, send_pass, bias_send, bias_recv):
+def stages(count):
+    out, stride = [], 1
+    while stride < count:
+        radix = 4 if count // stride % 4 == 0 else 2
+        out.append((stride, radix))
+        stride *= radix
+    return out
+
+
+def kernel(count, e_ref, member_ref, moved_ref, relative_ref, held, passing, bias, bias_col, sums, dens, density_row, totals,
+           recv, send_own, send_x, send_pass, bias_send, bias_recv, total_send, total_recv):
     rows, width = e_ref.shape
     chunks = rows // CHUNK
     half = chunks // 2
@@ -79,10 +88,16 @@
     diagonal = device(step, 1 - x)
     opposite = device(2, 1 - x)
 
+    peers = []
+    for stride, radix in stages(count):
+        digit = lax.rem(lax.div(me, stride), radix)
+        peers.append([me + (lax.rem(digit + d, radix) - digit) * stride for d in range(1, radix)])
+
     barrier = pltpu.get_barrier_semaphore()
-    for other in (ahead, behind, across, diagonal, opposite):
+    greeted = [ahead, behind, across, diagonal, opposite] + [other for line in peers for other in line]
+    for other in greeted:
         pl.semaphore_signal(barrier, inc=1, device_id={"gx": other}, device_id_type=MESH)
-    pl.semaphore_wait(barrier, 5)
+    pl.semaphore_wait(barrier, len(greeted))
 
     def piece(role, k):
         if role == 0:
@@ -206,10 +221,42 @@
     @pl.loop(0, rows // LANES)
     def _(i):
         at = pl.ds(pl.multiple_of(i * LANES, LANES), LANES)
-        density = jnp.sum(dens[at, :], axis=1, keepdims=True)
-        wide = jnp.broadcast_to(density, (LANES, LANES))
-        density_ref[:, at] = jnp.transpose(wide)[0:1, :]
-        moved_ref[at, :] = (sums[at, :] / jnp.maximum(density, 1.0)).astype(moved_ref.dtype)
+        density = jnp.broadcast_to(jnp.sum(dens[at, :], axis=1, keepdims=True), (LANES, LANES))
+        dens[at, :] = density
+        density_row[:, at] = jnp.transpose(density)[0:1, :]
+
+    def exchange(stage):
+        made = []
+        for d, other in enumerate(peers[stage], 1):
+            made.append(pltpu.make_async_remote_copy(
+                src_ref=totals.at[stage, 0], dst_ref=totals.at[stage, d], send_sem=total_send.at[stage, d - 1],
+                recv_sem=total_recv.at[stage, d - 1], device_id={"gx": other}, device_id_type=MESH))
+            made[-1].start()
+        return made
+
+    member = member_ref[...].astype(jnp.float32)
+    local_density = jnp.sum(density_row[...] * member, axis=1, keepdims=True)
+    local_count = jnp.sum(member, axis=1, keepdims=True)
+    first_line = lax.broadcasted_iota(jnp.int32, (8, LANES), 0) == 0
+    totals[0, 0] = jnp.where(first_line, jnp.broadcast_to(local_density, (8, LANES)), jnp.broadcast_to(local_count, (8, LANES)))
+    flying = exchange(0)
+
+    @pl.loop(0, rows // LANES)
+    def _(i):
+        at = pl.ds(pl.multiple_of(i * LANES, LANES), LANES)
+        moved_ref[at, :] = (sums[at, :] / jnp.maximum(dens[at, 0:1], 1.0)).astype(moved_ref.dtype)
+
+    for stage in range(len(peers)):
+        for made in flying:
+            made.wait()
+        total = totals[stage, 0]
+        for d in range(1, len(peers[stage]) + 1):
+            total = total + totals[stage, d]
+        if stage + 1 < len(peers):
+            totals[stage + 1, 0] = total
+            flying = exchange(stage + 1)
+    mean = total[0:1, 0:1] / jnp.maximum(total[1:2, 0:1], 1.0)
+    relative_ref[...] = density_row[...] / (1.0 + mean)
 
     for made in copies:
         made.wait_send()
@@ -219,7 +266,8 @@
     rows, width = embeddings.shape
     chunks = rows // CHUNK
     vmem = pl.BlockSpec(memory_space=pltpu.VMEM)
-    moved, density = pl.pallas_call(
+    count_stages = len(stages(count))
+    moved, relative = pl.pallas_call(
         functools.partial(kernel, count),
         out_shape=(jax.ShapeDtypeStruct((rows, width), jnp.bfloat16), jax.ShapeDtypeStruct((1, rows), jnp.float32)),
         in_specs=[vmem, vmem],
@@ -231,20 +279,20 @@
             pltpu.VMEM((rows, LANES), jnp.float32),
             pltpu.VMEM((rows, width), jnp.float32),
             pltpu.VMEM((rows, LANES), jnp.float32),
+            pltpu.VMEM((1, rows), jnp.float32),
+            pltpu.VMEM((count_stages, 4, 8, LANES), jnp.float32),
             pltpu.SemaphoreType.DMA((5, chunks)),
             pltpu.SemaphoreType.DMA((2, chunks)),
             pltpu.SemaphoreType.DMA((2, chunks)),
             pltpu.SemaphoreType.DMA((chunks,)),
             pltpu.SemaphoreType.DMA((4,)),
             pltpu.SemaphoreType.DMA((4,)),
+            pltpu.SemaphoreType.DMA((count_stages, 3)),
+            pltpu.SemaphoreType.DMA((count_stages, 3)),
         ],
         compiler_params=pltpu.CompilerParams(collective_id=0, has_side_effects=True, vmem_limit_bytes=48 * 1024 * 1024),
     )(embeddings, membership[None, :])
-    density = density[0]
-    member = membership.astype(jnp.float32)
-    member_density, member_count = lax.psum((jnp.sum(density * member), jnp.sum(member)), "gx")
-    relative = density / (1.0 + member_density / jnp.maximum(member_count, 1.0))
-    return (moved, relative)
+    return (moved, relative[0])
 
 
 def solution(mesh):

time: 155 us -> 128 us (0.83)
  blocking collectives: 30.1 us -> 0 us
  Pallas kernels: 118 us -> 124 us
    psum x1 -> x0, blocking collectives: 30.1 us -> none  [shards(): lax.psum((jnp.sum(density * member), jnp.sum(member)), 'gx')]
    pallas_call x1, Pallas kernels: 118 us -> 124 us  [shards(): pl.pallas_call(functools.partial(kernel, count), out_shape=(jax.ShapeDtyp...]
where the time goes in v2:
time: 128 us
  Pallas kernels  124 us (97%)
  local copies, waits for them, and re-layouts  3.24 us (3%)
    pallas_call x1, Pallas kernels, shards(): pl.pallas_call(functools.partial(kernel, count), out_shape=(jax.ShapeDtyp...  124 us

profile of v2, /device:TPU:0, one launch (start us, length us, event | category | flops | bytes accessed | tf_op | source)
XLA Modules:
  0.0 128.3 jit_solution(4207667559587860350)
XLA Ops:
  0.6 0.7 broadcast_in_dim.3.member_ref
  1.3 0.0 copy-start
  1.3 1.4 %copy-done = bf16[768,1024]{1,0:T(8,128)(2,1)S(1)} copy-done((bf16[768,1024]{1,0:T(8,128)(2,1)S(1)}, bf16[768,1024]{1,0:T(8,128)(2,1)}, u32[]{:S(2)}) %copy-start) | copy-done | bytes 1572888
  2.7 123.8 %shard_map.41 = (bf16[768,1024]{1,0:T(8,128)(2,1)S(1)}, f32[1,768]{1,0:T(1,128)S(1)}) custom-call(bf16[768,1024]{1,0:T(8,128)(2,1)S(1)} %copy-done, s32[1,768]{1,0:T(1,128)S(1)} %broadcast_in_dim.3.member_ref), custom_call_target="tpu_custom_call" | custom-call | tf_op jit(solution)/shard_map/pallas_call | solution.py:270
  126.5 0.6 reduce
  127.1 1.1 copy.5
Async XLA Ops:
  1.3 1.4 %copy-start = (bf16[768,1024]{1,0:T(8,128)(2,1)S(1)}, bf16[768,1024]{1,0:T(8,128)(2,1)}, u32[]{:S(2)}) copy-start(bf16[768,1024]{1,0:T(8,128)(2,1)} %e_ref.1) | copy-start | bytes 4718596

commit v3 on v2

v3 whole, which is shorter than its diff:
```python
import functools

import jax
import jax.numpy as jnp
from jax import lax
from jax.experimental import pallas as pl
from jax.experimental.pallas import tpu as pltpu
from jax.sharding import PartitionSpec as P

MESH = pl.DeviceIdType.MESH
CHUNK = 64
LAG = 2
TILE = 384
LANES = 128


def slot_of(stream, distance):
    return stream if distance == 1 else distance


def stages(count):
    out, stride = [], 1
    while stride < count:
        radix = 4 if count // stride % 4 == 0 else 2
        out.append((stride, radix))
        stride *= radix
    return out


def kernel(count, e_ref, member_ref, moved_ref, relative_ref, held, bias, bias_col, sums, dens, density_row, totals,
           recv, send_stream, send_x, bias_send, bias_recv, total_send, total_recv):
    rows, width = e_ref.shape
    chunks = rows // CHUNK
    tile = TILE if rows % TILE == 0 else rows
    scale = 4.0 / width
    unit = count // 8
    me = lax.axis_index("gx")
    z = lax.div(me, 2 * unit)
    x = lax.rem(lax.div(me, unit), 2)
    rest = lax.rem(me, unit)
    step = 1 - 2 * x

    def device(up, side):
        return (lax.rem(z + up + 4, 4) * 2 + side) * unit + rest

    above = device(1, x)
    below = device(-1, x)
    across = device(0, 1 - x)
    diagonal = device(step, 1 - x)
    opposite = device(2, 1 - x)

    peers = []
    for stride, radix in stages(count):
        digit = lax.rem(lax.div(me, stride), radix)
        peers.append([me + (lax.rem(digit + d, radix) - digit) * stride for d in range(1, radix)])

    barrier = pltpu.get_barrier_semaphore()
    greeted = [above, below, across, diagonal, opposite] + [other for line in peers for other in line]
    for other in greeted:
        pl.semaphore_signal(barrier, inc=1, device_id={"gx": other}, device_id_type=MESH)
    pl.semaphore_wait(barrier, len(greeted))

    def piece(slot, k):
        if slot is None:
            return e_ref.at[pl.ds(k * CHUNK, CHUNK)]
        return held.at[slot, pl.ds(k * CHUNK, CHUNK)]

    def copy(source, target, k, sem, other):
        return pltpu.make_async_remote_copy(
            src_ref=piece(source, k), dst_ref=piece(target, k), send_sem=sem, recv_sem=recv.at[target, k],
            device_id={"gx": other}, device_id_type=MESH)

    def exists(stream, distance):
        return z >= distance if stream == 0 else z <= 3 - distance

    def sends(stream, distance):
        return z < 4 - 1 if (stream, distance) == (0, 0) else z > 0 if (stream, distance) == (1, 0) else (
            jnp.logical_and(exists(stream, distance), z < 3 if stream == 0 else z > 0))

    def crosses(stream, distance):
        there = exists(stream, distance)
        if distance == 2:
            return there
        return jnp.logical_and(there, x == (stream if distance == 1 else 1 - stream))

    def crossing(stream, distance):
        there = exists(stream, distance)
        if distance == 2:
            return there
        return jnp.logical_and(there, x == (1 - stream if distance == 1 else stream))

    def stream_copy(stream, position):
        distance, k = position // chunks, position % chunks
        source = None if distance == 0 else slot_of(stream, distance)
        return copy(source, slot_of(stream, distance + 1), k, send_stream.at[stream, distance, k], above if stream == 0 else below)

    def cross_copy(stream, distance, k):
        side = 1 if distance == 2 else 0
        return copy(slot_of(stream, distance), 4 + side, k, send_x.at[side, k], across)

    def wait_slot(slot, k):
        copy(slot, slot, k, send_x.at[0, 0], across).wait_recv()

    def step_streams(t):
        for stream in (0, 1):
            position = t - LAG
            if 0 <= position < 3 * chunks:
                distance, k = position // chunks + 1, position % chunks

                @pl.when(exists(stream, distance))
                def _():
                    wait_slot(slot_of(stream, distance), k)

                @pl.when(crosses(stream, distance))
                def _():
                    cross_copy(stream, distance, k).start()

            if t < 3 * chunks:
                @pl.when(sends(stream, t // chunks))
                def _():
                    stream_copy(stream, t).start()

    def prepare():
        @pl.loop(0, rows // LANES)
        def _(i):
            at = pl.ds(pl.multiple_of(i * LANES, LANES), LANES)
            values = e_ref[at, :].astype(jnp.float32)
            norms = jnp.sum(values * values, axis=1, keepdims=True) * scale
            wide = jnp.broadcast_to(norms, (LANES, LANES))
            bias_col[at, :] = wide
            line = jnp.transpose(wide)[0:1, :]
            bias[0, :, at] = jnp.where(member_ref[:, at] > 0, line, 1e30)
            dens[at, :] = jnp.zeros((LANES, LANES), jnp.float32)

    def compute(slot, role, start, size, first=False):
        @pl.loop(0, rows // 256)
        def _(i):
            at = pl.ds(pl.multiple_of(i * 256, 256), 256)
            keys = e_ref[start:start + size, :] if slot is None else held[slot, start:start + size, :]
            dots = lax.dot_general(e_ref[at, :], keys, (((1,), (1,)), ((), ())), preferred_element_type=jnp.float32)
            own = bias_col[at, :]
            total = dens[at, :]
            parts = []
            for j in range(0, size, LANES):
                dist = own + bias[role, :, start + j:start + j + LANES]
                weight = jnp.exp(2.0 * scale * dots[:, j:j + LANES] - dist)
                total = total + weight
                parts.append(weight.astype(jnp.bfloat16))
            dens[at, :] = total
            low = jnp.concatenate(parts, axis=1) if len(parts) > 1 else parts[0]
            term = jnp.dot(low, keys, preferred_element_type=jnp.float32)
            if first:
                sums[at, :] = term
            else:
                sums[at, :] += term

    def bias_copy(role, other):
        return pltpu.make_async_remote_copy(
            src_ref=bias.at[0], dst_ref=bias.at[role], send_sem=bias_send.at[role - 1], recv_sem=bias_recv.at[role - 1],
            device_id={"gx": other}, device_id_type=MESH)

    def split(distance):
        if distance == 3 and rows == 768:
            return [(0, 384), (384, 256), (640, 128)]
        return [(start, tile) for start in range(0, rows, tile)]

    wrapped = jnp.where(z == 0, 1, 2)
    tiles = []
    for distance in (1, 2, 3):
        for start, size in split(distance):
            when = (distance - 1) * chunks + (start + size) // CHUNK - 1 + LAG
            either = jnp.logical_or(crossing(0, distance), crossing(1, distance))
            if distance == 1:
                tiles.append((when, exists(0, 1), 0, 1, start, size, False))
                tiles.append((when, exists(1, 1), 1, 2, start, size, False))
                tiles.append((when + LAG, either, 4, 3, start, size, True))
            elif distance == 2:
                tiles.append((when + LAG, None, 5, 4, start, size, True))
            else:
                tiles.append((when, jnp.logical_or(z == 0, z == 3), 3, wrapped, start, size, False))
                tiles.append((when + LAG, either, 4, 3, start, size, True))
    tiles.sort(key=lambda item: item[0])

    def run(item):
        _, condition, slot, role, start, size, crossed = item

        def body():
            if crossed:
                for k in range(start // CHUNK, (start + size) // CHUNK):
                    wait_slot(slot, k)
            compute(slot, role, start, size)

        if condition is None:
            body()
        else:
            pl.when(condition)(body)

    own_tiles = list(range(0, rows, tile))
    for t in range(LAG):
        step_streams(t)
    prepare()
    bias_copies = [bias_copy(role, other) for role, other in ((1, above), (2, below), (3, diagonal), (4, opposite))]
    for made in bias_copies:
        made.start()
    for t in range(LAG, 3 * chunks + LAG):
        step_streams(t)
        if own_tiles:
            start = own_tiles.pop(0)
            compute(None, 0, start, tile, first=start == 0)
            if not own_tiles:
                for made in bias_copies:
                    made.wait_recv()
            continue
        done = 0
        while tiles and tiles[0][0] <= t and done < 2:
            run(tiles.pop(0))
            done += 1
    for item in tiles:
        run(item)

    @pl.loop(0, rows // LANES)
    def _(i):
        at = pl.ds(pl.multiple_of(i * LANES, LANES), LANES)
        density = jnp.broadcast_to(jnp.sum(dens[at, :], axis=1, keepdims=True), (LANES, LANES))
        dens[at, :] = density
        density_row[:, at] = jnp.transpose(density)[0:1, :]

    def exchange(stage):
        made = []
        for d, other in enumerate(peers[stage], 1):
            made.append(pltpu.make_async_remote_copy(
                src_ref=totals.at[stage, 0], dst_ref=totals.at[stage, d], send_sem=total_send.at[stage, d - 1],
                recv_sem=total_recv.at[stage, d - 1], device_id={"gx": other}, device_id_type=MESH))
            made[-1].start()
        return made

    member = member_ref[...].astype(jnp.float32)
    local_density = jnp.sum(density_row[...] * member, axis=1, keepdims=True)
    local_count = jnp.sum(member, axis=1, keepdims=True)
    first_line = lax.broadcasted_iota(jnp.int32, (8, LANES), 0) == 0
    totals[0, 0] = jnp.where(first_line, jnp.broadcast_to(local_density, (8, LANES)), jnp.broadcast_to(local_count, (8, LANES)))
    flying = exchange(0)

    @pl.loop(0, rows // LANES)
    def _(i):
        at = pl.ds(pl.multiple_of(i * LANES, LANES), LANES)
        moved_ref[at, :] = (sums[at, :] / jnp.maximum(dens[at, 0:1], 1.0)).astype(moved_ref.dtype)

    for stage in range(len(peers)):
        for made in flying:
            made.wait()
        total = totals[stage, 0]
        for d in range(1, len(peers[stage]) + 1):
            total = total + totals[stage, d]
        if stage + 1 < len(peers):
            totals[stage + 1, 0] = total
            flying = exchange(stage + 1)
    mean = total[0:1, 0:1] / jnp.maximum(total[1:2, 0:1], 1.0)
    relative_ref[...] = density_row[...] / (1.0 + mean)

    for made in bias_copies:
        made.wait_send()
    for stream in (0, 1):
        for distance in range(3):
            @pl.when(sends(stream, distance))
            def _():
                for k in range(chunks):
                    stream_copy(stream, distance * chunks + k).wait_send()

            @pl.when(crosses(stream, distance + 1))
            def _():
                for k in range(chunks):
                    cross_copy(stream, distance + 1, k).wait_send()


def shards(count, embeddings, membership):
    rows, width = embeddings.shape
    chunks = rows // CHUNK
    vmem = pl.BlockSpec(memory_space=pltpu.VMEM)
    count_stages = len(stages(count))
    moved, relative = pl.pallas_call(
        functools.partial(kernel, count),
        out_shape=(jax.ShapeDtypeStruct((rows, width), jnp.bfloat16), jax.ShapeDtypeStruct((1, rows), jnp.float32)),
        in_specs=[vmem, vmem],
        out_specs=(vmem, vmem),
        scratch_shapes=[
            pltpu.VMEM((6, rows, width), jnp.bfloat16),
            pltpu.VMEM((5, 1, rows), jnp.float32),
            pltpu.VMEM((rows, LANES), jnp.float32),
            pltpu.VMEM((rows, width), jnp.float32),
            pltpu.VMEM((rows, LANES), jnp.float32),
            pltpu.VMEM((1, rows), jnp.float32),
            pltpu.VMEM((count_stages, 4, 8, LANES), jnp.float32),
            pltpu.SemaphoreType.DMA((6, chunks)),
            pltpu.SemaphoreType.DMA((2, 3, chunks)),
            pltpu.SemaphoreType.DMA((2, chunks)),
            pltpu.SemaphoreType.DMA((4,)),
            pltpu.SemaphoreType.DMA((4,)),
            pltpu.SemaphoreType.DMA((count_stages, 3)),
            pltpu.SemaphoreType.DMA((count_stages, 3)),
        ],
        compiler_params=pltpu.CompilerParams(collective_id=0, has_side_effects=True, vmem_limit_bytes=48 * 1024 * 1024),
    )(embeddings, membership[None, :])
    return (moved, relative[0])


def solution(mesh):
    in_specs = (P(("groups", "gx"), None), P(("groups", "gx")))
    out_specs = (P(("groups", "gx"), None), P(("groups", "gx")))
    step = functools.partial(shards, mesh.shape["gx"])
    return jax.shard_map(step, mesh=mesh, in_specs=in_specs, out_specs=out_specs, check_vma=False)
```

time: 128 us -> 131 us (1.023)
  Pallas kernels: 124 us -> 126 us
    pallas_call x1, Pallas kernels: 124 us -> 126 us  [shards(): pl.pallas_call(functools.partial(kernel, count), out_shape=(jax.ShapeDtyp...]
where the time goes in v3:
time: 131 us
  Pallas kernels  126 us (96%)
  local copies, waits for them, and re-layouts  3.24 us (2%)
    pallas_call x1, Pallas kernels, shards(): pl.pallas_call(functools.partial(kernel, count), out_shape=(jax.ShapeDtyp...  126 us

profile of v3, /device:TPU:0, one launch (start us, length us, event | category | flops | bytes accessed | tf_op | source)
XLA Modules:
  0.0 130.7 jit_solution(3860739260511152248)
XLA Ops:
  0.6 0.7 broadcast_in_dim.3.member_ref
  1.3 0.0 copy-start
  1.3 1.4 %copy-done = bf16[768,1024]{1,0:T(8,128)(2,1)S(1)} copy-done((bf16[768,1024]{1,0:T(8,128)(2,1)S(1)}, bf16[768,1024]{1,0:T(8,128)(2,1)}, u32[]{:S(2)}) %copy-start) | copy-done | bytes 1572888
  2.7 126.2 %shard_map.41 = (bf16[768,1024]{1,0:T(8,128)(2,1)S(1)}, f32[1,768]{1,0:T(1,128)S(1)}) custom-call(bf16[768,1024]{1,0:T(8,128)(2,1)S(1)} %copy-done, s32[1,768]{1,0:T(1,128)S(1)} %broadcast_in_dim.3.member_ref), custom_call_target="tpu_custom_call" | custom-call | tf_op jit(solution)/shard_map/pallas_call | solution.py:281
  128.9 0.6 reduce
  129.6 1.1 copy.5
Async XLA Ops:
  1.3 1.4 %copy-start = (bf16[768,1024]{1,0:T(8,128)(2,1)S(1)}, bf16[768,1024]{1,0:T(8,128)(2,1)}, u32[]{:S(2)}) copy-start(bf16[768,1024]{1,0:T(8,128)(2,1)} %e_ref.1) | copy-start | bytes 4718596

commit v4 on v3

--- a/solution.py
+++ b/solution.py
@@ -9,7 +9,7 @@
 
 MESH = pl.DeviceIdType.MESH
 CHUNK = 64
-LAG = 2
+LAG = 6
 TILE = 384
 LANES = 128
 

time: 131 us -> 130 us (level)
  no operation moved by 1% of the time
where the time goes in v4:
time: 130 us
  Pallas kernels  125 us (96%)
  local copies, waits for them, and re-layouts  3.24 us (2%)
    pallas_call x1, Pallas kernels, shards(): pl.pallas_call(functools.partial(kernel, count), out_shape=(jax.ShapeDtyp...  125 us

profile of v4, /device:TPU:0, one launch (start us, length us, event | category | flops | bytes accessed | tf_op | source)
XLA Modules:
  0.0 129.7 jit_solution(826825566075989700)
XLA Ops:
  0.6 0.7 broadcast_in_dim.3.member_ref
  1.3 0.0 copy-start
  1.3 1.4 %copy-done = bf16[768,1024]{1,0:T(8,128)(2,1)S(1)} copy-done((bf16[768,1024]{1,0:T(8,128)(2,1)S(1)}, bf16[768,1024]{1,0:T(8,128)(2,1)}, u32[]{:S(2)}) %copy-start) | copy-done | bytes 1572888
  2.7 125.2 %shard_map.41 = (bf16[768,1024]{1,0:T(8,128)(2,1)S(1)}, f32[1,768]{1,0:T(1,128)S(1)}) custom-call(bf16[768,1024]{1,0:T(8,128)(2,1)S(1)} %copy-done, s32[1,768]{1,0:T(1,128)S(1)} %broadcast_in_dim.3.member_ref), custom_call_target="tpu_custom_call" | custom-call | tf_op jit(solution)/shard_map/pallas_call | solution.py:281
  127.9 0.6 reduce
  128.6 1.1 copy.5
Async XLA Ops:
  1.3 1.4 %copy-start = (bf16[768,1024]{1,0:T(8,128)(2,1)S(1)}, bf16[768,1024]{1,0:T(8,128)(2,1)}, u32[]{:S(2)}) copy-start(bf16[768,1024]{1,0:T(8,128)(2,1)} %e_ref.1) | copy-start | bytes 4718596
